TPU v7x, 128 devices: a whole 4x4x4 slice. The times are simulated.
128 devices in a mesh: node: 16 (over x_hi, y, core), local: 8 (over z, x_lo).
Axes of the slice: x: 4 (x_hi: 2, x_lo: 2; x = x_hi * 2 + x_lo), y: 4, z: 4, core: 2. Of those that a mesh axis runs over, the one named last changes fastest.
Arguments:
- output_grad: bfloat16 [65536, 768], P(('node', 'local')), may hold values from -6 to 6
- gate_prob: float32 [65536], P(('node', 'local')), may hold values from 0.2 to 1
- expert_ids: int32 [65536], P(('node', 'local')), may hold values from 0 to 127, as said below
- slots: int32 [65536], P(('node', 'local')), may hold values from -1 to 4, as said below
- expert_inputs: bfloat16 [128, 640, 768], P(('node', 'local')), may hold values from -6 to 6
- w_in: bfloat16 [128, 768, 3072], P(('node', 'local')), may hold values from -0.21875 to 0.21875
- w_out: bfloat16 [128, 3072, 768], P(('node', 'local')), may hold values from -0.109375 to 0.109375
Outputs:
- token_grad: bfloat16 [65536, 768], P(('node', 'local'))
- gate_grad: float32 [65536], P(('node', 'local'))
- w_in_grad: bfloat16 [128, 768, 3072], P(('node', 'local'))
- w_out_grad: bfloat16 [128, 3072, 768], P(('node', 'local'))
Inputs may be any that keep to these rules, and one draw needn't show every extreme that they name: `expert_ids`: on every device some expert (the same on all devices) is chosen by more than 5 of its tokens. slots[t] counts the earlier tokens of the same device with the same expert; tokens with count 5 or more are dropped and have -1. On every device some token takes slot 4, the last of its expert's 5 slots.
All inputs are finite; a program needn't handle non-finite values.
Results may differ from a plain program's by a relative error of at most 0.0058.
Values may be sent and summed in bfloat16 or wider, within the bound.
A program may use at most 128 MiB of HBM per device.

v0:
```python
import math

import jax
import jax.numpy as jnp
from jax import lax
from jax.sharding import PartitionSpec as P


def normal_parts(pre):
    cdf = 0.5 * (1.0 + jax.scipy.special.erf(pre / math.sqrt(2.0)))
    dens = jnp.exp(-0.5 * pre * pre) / math.sqrt(2.0 * math.pi)
    return (cdf, dens)


def shards(output_grad, gate_prob, expert_ids, slots, expert_inputs, w_in, w_out):
    n_node = lax.axis_size("node")
    n_local = lax.axis_size("local")
    n_experts = n_node * n_local
    rows = expert_inputs.shape[1]
    cap = rows // n_experts
    width = output_grad.shape[1]
    keep = slots >= 0
    target = jnp.where(keep, expert_ids * cap + slots, n_experts * cap)
    outgoing = (gate_prob[:, None] * output_grad.astype(jnp.float32)).astype(jnp.bfloat16)
    buffer = jnp.zeros((n_experts * cap, width), jnp.bfloat16).at[target].set(outgoing, mode="drop")
    received = lax.all_to_all(
        buffer.reshape(n_experts, cap, width),
        ("node", "local"),
        split_axis=0,
        concat_axis=0,
        tiled=True,
    )
    grad_plain = received.reshape(rows, width)
    inputs = expert_inputs[0]
    weight_in = w_in[0]
    weight_out = w_out[0]
    pre = jnp.dot(inputs, weight_in, preferred_element_type=jnp.float32)
    cdf, dens = normal_parts(pre)
    hidden = (pre * cdf).astype(jnp.bfloat16)
    expert_out = jnp.dot(hidden, weight_out, preferred_element_type=jnp.float32).astype(
        jnp.bfloat16
    )
    hidden_grad = lax.dot_general(
        grad_plain, weight_out, (((1,), (1,)), ((), ())), preferred_element_type=jnp.float32
    )
    pre_grad = (hidden_grad * (cdf + pre * dens)).astype(jnp.bfloat16)
    input_grad = lax.dot_general(
        pre_grad, weight_in, (((1,), (1,)), ((), ())), preferred_element_type=jnp.float32
    ).astype(jnp.bfloat16)
    picked = jnp.minimum(target, n_experts * cap - 1)
    back_grad = lax.all_to_all(
        input_grad.reshape(n_experts, cap, width),
        ("node", "local"),
        split_axis=0,
        concat_axis=0,
        tiled=True,
    )
    back_out = lax.all_to_all(
        expert_out.reshape(n_experts, cap, width),
        ("node", "local"),
        split_axis=0,
        concat_axis=0,
        tiled=True,
    )
    out_rows = back_out.reshape(n_experts * cap, width)[picked]
    product = jnp.sum(output_grad.astype(jnp.float32) * out_rows.astype(jnp.float32), axis=1)
    out_grad = lax.dot_general(
        hidden, grad_plain, (((0,), (0,)), ((), ())), preferred_element_type=jnp.float32
    ).astype(jnp.bfloat16)
    in_grad = lax.dot_general(
        inputs, pre_grad, (((0,), (0,)), ((), ())), preferred_element_type=jnp.float32
    ).astype(jnp.bfloat16)
    grad_rows = back_grad.reshape(n_experts * cap, width)[picked]
    token_grad = jnp.where(keep[:, None], grad_rows, jnp.zeros_like(grad_rows))
    gate_grad = jnp.where(keep, product, jnp.float32(0.0))
    return (token_grad, gate_grad, in_grad[None], out_grad[None])


def solution(mesh):
    placed = (
        P(("node", "local"), None),
        P(("node", "local")),
        P(("node", "local")),
        P(("node", "local")),
        P(("node", "local"), None, None),
        P(("node", "local"), None, None),
        P(("node", "local"), None, None),
    )
    return jax.shard_map(
        shards,
        mesh=mesh,
        in_specs=placed,
        out_specs=(
            P(("node", "local"), None),
            P(("node", "local")),
            P(("node", "local"), None, None),
            P(("node", "local"), None, None),
        ),
        check_vma=False,
    )
```

profile of v0, /device:TPU:1, one launch (start us, length us, event | category | flops | bytes accessed | tf_op | source)
XLA Modules:
  0.0 117.5 jit_solution(5778921786743013031)
XLA Ops:
  0.6 0.0 copy-start
  0.6 0.8 compare_select_fusion
  1.4 0.7 compare_select_fusion.1
  2.1 3.6 %scatter_custom_fusion = bf16[640,768]{1,0:T(8,128)(2,1)S(1)} fusion(s32[512]{0:T(512)S(1)} %compare_select_fusion.1, bf16[512,768]{1,0:T(8,128)(2,1)} %param.7, f32[512]{0:T(512)} %param.8, bf16[]{:T(256)} %constant.12.clone.1), kind=kCustom, calls=%fused_computation.31 | custom fusion | flops 1179648 | bytes 1771522 | tf_op jit(solution)/shard_map/scatter | solution.py:25
  5.8 1.3 %reshape.28 = bf16[128,5,768]{2,1,0:T(8,128)(2,1)} reshape(bf16[640,768]{1,0:T(8,128)(2,1)S(1)} %scatter_custom_fusion) | data formatting | bytes 1966080 | tf_op jit(solution)/shard_map/reshape | solution.py:27
  7.1 11.5 %all-to-all-start = ((bf16[128,5,768]{2,1,0:T(8,128)(2,1)}), bf16[128,5,768]{2,1,0:T(8,128)(2,1)S(1)}, u32[]{:S(2)}, u32[]{:S(2)}) async-start(bf16[128,5,768]{2,1,0:T(8,128)(2,1)} %reshape.28), calls=%async_computation | async-start | bytes 3145728 | tf_op jit(solution)/shard_map/all_to_all | solution.py:26
  18.6 0.0 copy-done
  18.6 7.2 %multiply_convert_fusion = (bf16[640,3072]{1,0:T(8,128)(2,1)S(1)}, f32[640,3072]{1,0:T(8,128)}) fusion(bf16[1,768,3072]{2,1,0:T(8,128)(2,1)} %param.12, bf16[1,640,768]{2,1,0:T(8,128)(2,1)S(1)} %copy-done), kind=kOutput, calls=%fused_computation.10 | convolution fusion | flops 3029729280 | bytes 17498112 | tf_op jit(solution)/shard_map/dot_general | solution.py:37
  25.8 0.0 copy-start.5
  25.8 2.0 %copy-done.5 = bf16[640,3072]{1,0:T(8,128)(2,1)} copy-done((bf16[640,3072]{1,0:T(8,128)(2,1)}, bf16[640,3072]{1,0:T(8,128)(2,1)S(1)}, u32[]{:S(2)}) %copy-start.5) | copy-done | bytes 3932184
  27.8 5.5 %fusion.17 = bf16[640,768]{1,0:T(8,128)(2,1)S(1)} fusion(bf16[640,3072]{1,0:T(8,128)(2,1)S(1)} %get-tuple-element.14, bf16[1,3072,768]{2,1,0:T(8,128)(2,1)} %param.13), kind=kOutput, calls=%fused_computation.27 | convolution fusion | flops 3020390400 | bytes 9633792 | tf_op jit(solution)/shard_map/dot_general | solution.py:40
  33.4 1.4 %reshape.32 = bf16[128,5,768]{2,1,0:T(8,128)(2,1)} reshape(bf16[640,768]{1,0:T(8,128)(2,1)S(1)} %fusion.17) | data formatting | bytes 1966080 | tf_op jit(solution)/shard_map/reshape | solution.py:59
  34.8 7.4 %all-to-all-done = bf16[128,5,768]{2,1,0:T(8,128)(2,1)S(1)} async-done(((bf16[128,5,768]{2,1,0:T(8,128)(2,1)}), bf16[128,5,768]{2,1,0:T(8,128)(2,1)S(1)}, u32[]{:S(2)}, u32[]{:S(2)}) %all-to-all-start) | async-done | bytes 983072 | tf_op jit(solution)/shard_map/all_to_all | solution.py:26
  42.3 0.0 copy-start.1
  42.3 1.1 copy-done.1
  43.4 5.7 %all-to-all-start.2 = ((bf16[128,5,768]{2,1,0:T(8,128)(2,1)}), bf16[128,5,768]{2,1,0:T(8,128)(2,1)S(1)}, u32[]{:S(2)}, u32[]{:S(2)}) async-start(bf16[128,5,768]{2,1,0:T(8,128)(2,1)} %reshape.32), calls=%async_computation.2 | async-start | bytes 3145728 | tf_op jit(solution)/shard_map/all_to_all | solution.py:58
  49.1 2.3 %reshape.29 = bf16[640,768]{1,0:T(8,128)(2,1)S(1)} reshape(bf16[128,5,768]{2,1,0:T(8,128)(2,1)} %copy-done.1) | data formatting | bytes 1966080 | tf_op jit(solution)/shard_map/reshape | solution.py:33
  51.4 0.0 copy-start.3
  51.4 8.1 %fusion.5 = bf16[640,3072]{1,0:T(8,128)(2,1)S(1)} fusion(f32[640,3072]{1,0:T(8,128)} %get-tuple-element.15, bf16[640,768]{1,0:T(8,128)(2,1)S(1)} %reshape.29, bf16[1,3072,768]{2,1,0:T(8,128)(2,1)} %param.13), kind=kOutput, calls=%fused_computation.9 | convolution fusion | flops 3039559680 | bytes 17498112 | tf_op jit(solution)/shard_map/dot_general | solution.py:43
  59.6 0.0 copy-done.3
  59.6 0.0 copy-start.6
  59.6 1.9 %copy-done.6 = bf16[640,3072]{1,0:T(8,128)(2,1)} copy-done((bf16[640,3072]{1,0:T(8,128)(2,1)}, bf16[640,3072]{1,0:T(8,128)(2,1)S(1)}, u32[]{:S(2)}) %copy-start.6) | copy-done | bytes 3932184
  61.5 6.6 %fusion.20 = bf16[640,768]{1,0:T(8,128)(2,1)} fusion(bf16[640,3072]{1,0:T(8,128)(2,1)S(1)} %fusion.5, bf16[1,768,3072]{2,1,0:T(8,128)(2,1)} %param.12), kind=kOutput, calls=%fused_computation.28 | convolution fusion | flops 3020390400 | bytes 9633792 | tf_op jit(solution)/shard_map/dot_general | solution.py:47
  68.1 3.0 %reshape.30 = bf16[128,5,768]{2,1,0:T(8,128)(2,1)} reshape(bf16[640,768]{1,0:T(8,128)(2,1)} %fusion.20) | data formatting | bytes 1966080 | tf_op jit(solution)/shard_map/reshape | solution.py:52
  71.1 7.6 %fusion.13 = bf16[1,768,3072]{1,2,0:T(8,128)(2,1)} fusion(bf16[640,3072]{1,0:T(8,128)(2,1)} %copy-done.6, bf16[1,640,768]{2,1,0:T(8,128)(2,1)S(1)} %copy-done), kind=kOutput, calls=%fused_computation.21 | convolution fusion | flops 3022258176 | bytes 9633792 | tf_op jit(solution)/shard_map/dot_general | solution.py:70
  78.7 0.0 all-to-all-done.2
  78.7 10.2 %all-to-all-start.1 = ((bf16[128,5,768]{2,1,0:T(8,128)(2,1)}), bf16[128,5,768]{2,1,0:T(8,128)(2,1)}, u32[]{:S(2)}, u32[]{:S(2)}) async-start(bf16[128,5,768]{2,1,0:T(8,128)(2,1)} %reshape.30), calls=%async_computation.1 | async-start | bytes 3145728 | tf_op jit(solution)/shard_map/all_to_all | solution.py:51
  88.8 0.5 reshape.33
  89.3 0.0 copy-start.2
  89.3 2.0 %gather_fusion.1 = bf16[512,768]{1,0:T(8,128)(2,1)S(1)} fusion(bf16[640,768]{1,0:T(8,128)(2,1)S(1)} %reshape.33, s32[1024]{0:T(1024)S(1)} %pad_clamp_fusion), kind=kCustom, calls=%fused_computation.1 | custom fusion | bytes 1574912 | tf_op jit(solution)/shard_map/gather | solution.py:65
  91.4 0.0 copy-done.2
  91.4 0.3 fusion.16
  91.6 0.0 copy-start.4
  91.6 6.7 %copy.12 = bf16[1,768,3072]{2,1,0:T(8,128)(2,1)} copy(bf16[1,768,3072]{1,2,0:T(8,128)(2,1)} %fusion.13) | data formatting | bytes 9437184
  98.3 0.6 broadcast_select_fusion.1
  98.9 0.0 copy-done.4
  98.9 7.6 %fusion.14 = bf16[1,3072,768]{2,1,0:T(8,128)(2,1)} fusion(bf16[640,3072]{1,0:T(8,128)(2,1)} %copy-done.5, bf16[640,768]{1,0:T(8,128)(2,1)S(1)} %copy-done.4), kind=kOutput, calls=%fused_computation.22 | convolution fusion | flops 3022258176 | bytes 9633792 | tf_op jit(solution)/shard_map/dot_general | solution.py:67
  106.6 5.6 %all-to-all-done.1 = bf16[128,5,768]{2,1,0:T(8,128)(2,1)} async-done(((bf16[128,5,768]{2,1,0:T(8,128)(2,1)}), bf16[128,5,768]{2,1,0:T(8,128)(2,1)}, u32[]{:S(2)}, u32[]{:S(2)}) %all-to-all-start.1) | async-done | bytes 983072 | tf_op jit(solution)/shard_map/all_to_all | solution.py:51
  112.2 2.3 %reshape.31 = bf16[640,768]{1,0:T(8,128)(2,1)S(1)} reshape(bf16[128,5,768]{2,1,0:T(8,128)(2,1)} %all-to-all-done.1) | data formatting | bytes 1966080 | tf_op jit(solution)/shard_map/reshape | solution.py:73
  114.5 2.0 %gather_fusion = bf16[512,768]{1,0:T(8,128)(2,1)S(1)} fusion(bf16[640,768]{1,0:T(8,128)(2,1)S(1)} %reshape.31, s32[1024]{0:T(1024)S(1)} %pad_clamp_fusion), kind=kCustom, calls=%fused_computation | custom fusion | bytes 1574912 | tf_op jit(solution)/shard_map/gather | solution.py:73
  116.5 1.0 broadcast_select_fusion
  (1 shorter events, 0.0 us)
Async XLA Ops:
  0.6 18.0 %copy-start = (bf16[1,640,768]{2,1,0:T(8,128)(2,1)S(1)}, bf16[1,640,768]{2,1,0:T(8,128)(2,1)}, u32[]{:S(2)}) copy-start(bf16[1,640,768]{2,1,0:T(8,128)(2,1)} %param.11) | copy-start | bytes 2949124
  7.1 35.1 %all-to-all-start = ((bf16[128,5,768]{2,1,0:T(8,128)(2,1)}), bf16[128,5,768]{2,1,0:T(8,128)(2,1)S(1)}, u32[]{:S(2)}, u32[]{:S(2)}) async-start(bf16[128,5,768]{2,1,0:T(8,128)(2,1)} %reshape.28), calls=%async_computation | async-start | bytes 3145728 | tf_op jit(solution)/shard_map/all_to_all | solution.py:26
  25.8 2.0 %copy-start.5 = (bf16[640,3072]{1,0:T(8,128)(2,1)}, bf16[640,3072]{1,0:T(8,128)(2,1)S(1)}, u32[]{:S(2)}) copy-start(bf16[640,3072]{1,0:T(8,128)(2,1)S(1)} %get-tuple-element.14) | copy-start | bytes 11796484
  42.3 1.1 copy-start.1
  43.4 35.3 %all-to-all-start.2 = ((bf16[128,5,768]{2,1,0:T(8,128)(2,1)}), bf16[128,5,768]{2,1,0:T(8,128)(2,1)S(1)}, u32[]{:S(2)}, u32[]{:S(2)}) async-start(bf16[128,5,768]{2,1,0:T(8,128)(2,1)} %reshape.32), calls=%async_computation.2 | async-start | bytes 3145728 | tf_op jit(solution)/shard_map/all_to_all | solution.py:58
  51.4 8.2 %copy-start.3 = (bf16[640,768]{1,0:T(8,128)(2,1)}, bf16[640,768]{1,0:T(8,128)(2,1)S(1)}, u32[]{:S(2)}) copy-start(bf16[640,768]{1,0:T(8,128)(2,1)S(1)} %reshape.29) | copy-start | bytes 2949124
  59.6 1.9 %copy-start.6 = (bf16[640,3072]{1,0:T(8,128)(2,1)}, bf16[640,3072]{1,0:T(8,128)(2,1)S(1)}, u32[]{:S(2)}) copy-start(bf16[640,3072]{1,0:T(8,128)(2,1)S(1)} %fusion.5) | copy-start | bytes 11796484
  78.7 33.5 %all-to-all-start.1 = ((bf16[128,5,768]{2,1,0:T(8,128)(2,1)}), bf16[128,5,768]{2,1,0:T(8,128)(2,1)}, u32[]{:S(2)}, u32[]{:S(2)}) async-start(bf16[128,5,768]{2,1,0:T(8,128)(2,1)} %reshape.30), calls=%async_computation.1 | async-start | bytes 3145728 | tf_op jit(solution)/shard_map/all_to_all | solution.py:51
  89.3 2.0 %copy-start.2 = (bf16[512,768]{1,0:T(8,128)(2,1)S(1)}, bf16[512,768]{1,0:T(8,128)(2,1)}, u32[]{:S(2)}) copy-start(bf16[512,768]{1,0:T(8,128)(2,1)} %param.7) | copy-start | bytes 2359300
  91.6 7.3 %copy-start.4 = (bf16[640,768]{1,0:T(8,128)(2,1)S(1)}, bf16[640,768]{1,0:T(8,128)(2,1)}, u32[]{:S(2)}) copy-start(bf16[640,768]{1,0:T(8,128)(2,1)} %copy-done.3) | copy-start | bytes 2949124
where the time goes:
time: 119 us; the launch traced here: 118 us
  matrix products  42.7 us (36%)
  starting transfers between devices  27.3 us (23%)
  local copies, waits for them, and re-layouts  26.6 us (22%)
  waiting for transfers between devices  13.1 us (11%)
  other arithmetic  7.01 us (6%)
    unnamed x15, local copies, waits for them, and re-layouts  11.7 us
    all_to_all x1, starting transfers between devices, shards(): lax.all_to_all(buffer.reshape(n_experts, cap, width), ('node', 'local'),...  11.5 us
    all_to_all x1, starting transfers between devices, shards(): lax.all_to_all(input_grad.reshape(n_experts, cap, width), ('node', 'local...  10.2 us
    dot_general x1, matrix products, shards(): lax.dot_general(grad_plain, weight_out, (((1,), (1,)), ((), ())), preferr...  8.14 us
    dot_general x1, matrix products, shards(): lax.dot_general(hidden, grad_plain, (((0,), (0,)), ((), ())), preferred_e...  7.63 us
    dot_general x1, matrix products, shards(): lax.dot_general(inputs, pre_grad, (((0,), (0,)), ((), ())), preferred_ele...  7.63 us
    all_to_all x1, waiting for transfers between devices, shards(): lax.all_to_all(buffer.reshape(n_experts, cap, width), ('node', 'local'),...  7.45 us
    dot_general x1, matrix products, shards(): pre = jnp.dot(inputs, weight_in, preferred_element_type=jnp.float32)  7.2 us
  transfers between devices with their start and end apart: 3, of which 2 were waited for; matrix products, arithmetic and copies ran while one was open for 51% of the time, Pallas kernels for 0%

commit v1 on v0

v1 whole, which is shorter than its diff:
```python
import functools
import math

import jax
import jax.numpy as jnp
from jax import lax
from jax.experimental import pallas as pl
from jax.experimental.pallas import tpu as pltpu
from jax.sharding import PartitionSpec as P

MESH = pl.DeviceIdType.MESH
F32 = jnp.float32
BF16 = jnp.bfloat16
LANES = 128
MSG = 32
NT = (((1,), (1,)), ((), ()))
TN = (((0,), (0,)), ((), ()))
VMEM_LIMIT = 60 * 1024 * 1024


def signal(sem, device):
    pl.semaphore_signal(sem, inc=1, device_id=device, device_id_type=MESH)


def exchange_kernel(
    n_node, n_local, cap, ids, slots, gate, og_hbm, x_hbm, win_hbm, wout_hbm,
    back, hid_t_hbm, pg_hbm, x_t_hbm, routed_hbm,
    og, x, win, wout, xp, x_t, hid, hid_t, slope, pg, routed, wide, msg, recv, ret,
    in_sem, out_sem, own_sem, send_sem, recv_sem, back_send_sem, back_recv_sem,
):
    node, local = lax.axis_index("node"), lax.axis_index("local")
    n_dev = n_node * n_local
    me = node * n_local + local
    core, pair = node % 2, node // 2
    n_pair = n_node // 2
    part = n_pair * n_local
    place = pair * n_local + local
    rows, width = xp.shape
    half = part * cap
    blocks = width // LANES
    ff = hid.shape[1]

    loads = [
        pltpu.make_async_copy(src, dst, in_sem.at[k])
        for k, (src, dst) in enumerate(((og_hbm, og), (x_hbm, x), (win_hbm, win), (wout_hbm, wout)))
    ]
    for load in loads:
        load.start()

    barrier = pltpu.get_barrier_semaphore()

    def greet(k, carry):
        for j in range(n_local):
            signal(barrier, ((node + k) % n_node, j))
        return carry

    lax.fori_loop(1, n_node, greet, 0)
    for j in range(1, n_local):
        signal(barrier, (node, (local + j) % n_local))

    loads[0].wait()
    target = jnp.where(slots[...] >= 0, slots[...] * n_dev + ids[...], -1)
    tokens = target.shape[1]
    for c in range(cap):
        hit = lax.broadcasted_iota(jnp.int32, (n_dev, tokens), 0) + c * n_dev == target
        moved = jnp.dot(hit.astype(BF16), og[...], preferred_element_type=F32)
        factor = jnp.sum(jnp.where(hit, gate[...], 0.0), axis=1, keepdims=True)
        moved = moved * factor
        for b in range(blocks):
            wide[pl.ds(c * blocks + b, n_dev, stride=MSG), :] = moved[:, b * LANES : (b + 1) * LANES]
    msg[...] = wide[...].reshape(n_dev, MSG, LANES).astype(BF16)

    pl.semaphore_wait(barrier, n_dev - 1)

    def peer(step, k):
        there = (place + k) % part
        return 2 * (there // n_local) + (core + step) % 2, there % n_local, there

    own = pltpu.make_async_copy(msg.at[me], recv.at[0, place], own_sem)
    own.start()
    for step in range(2):

        def send(k, carry, step=step):
            to_node, to_local, there = peer(step, k)
            pltpu.make_async_remote_copy(
                src_ref=msg.at[to_node * n_local + to_local],
                dst_ref=recv.at[step, place],
                send_sem=send_sem,
                recv_sem=recv_sem.at[step],
                device_id=(to_node, to_local),
                device_id_type=MESH,
            ).start()
            return carry

        lax.fori_loop(1 - step, part, send, 0)

    loads[1].wait()
    for step in range(2):
        r = lax.broadcasted_iota(jnp.int32, (half, rows), 0)
        c, i = r // part, r % part
        source = (i // n_local) * (2 * n_local) + ((core + step) % 2) * n_local + i % n_local
        hit = lax.broadcasted_iota(jnp.int32, (half, rows), 1) == source * cap + c
        ordered = jnp.dot(hit.astype(BF16), x[...], preferred_element_type=F32).astype(BF16)
        xp[step * half : (step + 1) * half, :] = ordered

    loads[2].wait()
    tile = 256

    def forward(k, carry):
        cols = pl.ds(pl.multiple_of(k * tile, tile), tile)
        pre = jnp.dot(xp[...], win[:, cols], preferred_element_type=F32)
        cdf = 0.5 * (1.0 + lax.erf(pre * (1.0 / math.sqrt(2.0))))
        dens = jnp.exp(-0.5 * pre * pre) * (1.0 / math.sqrt(2.0 * math.pi))
        hidden = (pre * cdf).astype(BF16)
        hid[:, cols] = hidden
        hid_t[cols, :] = hidden.T
        slope[:, cols] = cdf + pre * dens
        return carry

    lax.fori_loop(0, ff // tile, forward, 0)
    x_t[...] = xp[...].T
    stores = [
        pltpu.make_async_copy(src, dst, out_sem.at[k])
        for k, (src, dst) in enumerate(
            ((hid_t, hid_t_hbm), (x_t, x_t_hbm), (pg, pg_hbm), (routed, routed_hbm))
        )
    ]
    stores[0].start()
    stores[1].start()
    own.wait()
    loads[3].wait()

    own_back = pltpu.make_async_copy(ret.at[0, place], back.at[me], own_sem)
    for step in range(2):
        mine = slice(step * half, (step + 1) * half)
        n_in = part - 1 + step
        got = recv.at[step, pl.ds(0, n_in)]
        pltpu.make_async_copy(got, got, recv_sem.at[step]).wait()
        wide[0 : part * MSG, :] = recv[step].astype(F32).reshape(part * MSG, LANES)
        for c in range(cap):
            for b in range(blocks):
                routed[step * half + c * part : step * half + (c + 1) * part, b * LANES : (b + 1) * LANES] = (
                    wide[pl.ds(c * blocks + b, part, stride=MSG), :].astype(BF16)
                )

        def backward(k, total, mine=mine):
            cols = pl.ds(pl.multiple_of(k * tile, tile), tile)
            up = lax.dot_general(routed[mine, :], wout[cols, :], NT, preferred_element_type=F32)
            pg[mine, cols] = (up * slope[mine, cols]).astype(BF16)
            both = up * hid[mine, cols].astype(F32)
            for b in range(tile // LANES):
                total = total + both[:, b * LANES : (b + 1) * LANES]
            return total

        total = lax.fori_loop(0, ff // tile, backward, jnp.zeros((half, LANES), F32))
        product = jnp.sum(total, axis=1, keepdims=True)
        lane = lax.broadcasted_iota(jnp.int32, (part, LANES), 1)
        spread = jnp.zeros((part, LANES), F32)
        for c in range(cap):
            spread = jnp.where(lane == c, product[c * part : (c + 1) * part], spread)
        high = spread.astype(BF16).astype(F32)
        wide[pl.ds(cap * blocks, part, stride=MSG), :] = high
        wide[pl.ds(cap * blocks + 1, part, stride=MSG), :] = spread - high
        for q in range(width // 256):
            down = lax.dot_general(
                pg[mine, :], win[q * 256 : (q + 1) * 256, :], NT, preferred_element_type=F32
            )
            for c in range(cap):
                for b in range(2):
                    wide[pl.ds(c * blocks + 2 * q + b, part, stride=MSG), :] = down[
                        c * part : (c + 1) * part, b * LANES : (b + 1) * LANES
                    ]
        ret[step] = wide[0 : part * MSG, :].reshape(part, MSG, LANES).astype(BF16)
        if step == 0:
            own_back.start()

        def reply(k, carry, step=step):
            to_node, to_local, there = peer(step, k)
            pltpu.make_async_remote_copy(
                src_ref=ret.at[step, there],
                dst_ref=back.at[me],
                send_sem=back_send_sem,
                recv_sem=back_recv_sem,
                device_id=(to_node, to_local),
                device_id_type=MESH,
            ).start()
            return carry

        lax.fori_loop(1 - step, part, reply, 0)

    stores[2].start()
    stores[3].start()
    sent = msg.at[pl.ds(0, n_dev - 1)]
    pltpu.make_async_copy(sent, sent, send_sem).wait()
    pltpu.make_async_copy(sent, sent, back_send_sem).wait()
    came = back.at[pl.ds(0, n_dev - 1)]
    own_back.wait()
    for store in stores:
        store.wait()
    pltpu.make_async_copy(came, came, back_recv_sem).wait()


def weights_kernel(
    cap, ids, slots, gate, back, hid_t, pg, x_t, routed, token_grad, gate_grad, in_grad, out_grad, wide, rows_back
):
    out_grad[...] = jnp.dot(hid_t[...], routed[...], preferred_element_type=F32).astype(BF16)
    in_grad[...] = jnp.dot(x_t[...], pg[...], preferred_element_type=F32).astype(BF16)

    @pl.when(pl.program_id(0) == 0)
    def _():
        n_dev = back.shape[0]
        tokens, width = token_grad.shape
        blocks = width // LANES
        wide[...] = back[...].astype(F32).reshape(n_dev * MSG, LANES)
        for c in range(cap):
            for b in range(blocks):
                rows_back[c * n_dev : (c + 1) * n_dev, b * LANES : (b + 1) * LANES] = wide[
                    pl.ds(c * blocks + b, n_dev, stride=MSG), :
                ].astype(BF16)
        high = wide[pl.ds(cap * blocks, n_dev, stride=MSG), :].astype(BF16)
        low = wide[pl.ds(cap * blocks + 1, n_dev, stride=MSG), :].astype(BF16)
        target = jnp.where(slots[...] >= 0, slots[...] * n_dev + ids[...], -1)
        column = jnp.broadcast_to(target.astype(F32), (LANES, tokens)).T
        lane = lax.broadcasted_iota(jnp.int32, (tokens, LANES), 1).astype(F32)
        hits = [
            jnp.where(column == lane + (k * LANES), 1.0, 0.0).astype(BF16)
            for k in range(cap * n_dev // LANES)
        ]
        token_grad[...] = jnp.dot(
            jnp.concatenate(hits, axis=1), rows_back[...], preferred_element_type=F32
        ).astype(BF16)
        expert = lax.broadcasted_iota(jnp.int32, (n_dev, tokens), 0) == ids[...]
        expert = expert.astype(BF16)
        products = lax.dot_general(high, expert, TN, preferred_element_type=F32)
        products += lax.dot_general(low, expert, TN, preferred_element_type=F32)
        chosen = lax.broadcasted_iota(jnp.int32, (LANES, tokens), 0) == slots[...]
        picked = jnp.sum(jnp.where(chosen, products, 0.0)[0:8], axis=0, keepdims=True)
        gate_grad[...] = picked / gate[...]


def shards(output_grad, gate_prob, expert_ids, slots, expert_inputs, w_in, w_out):
    n_node = lax.axis_size("node")
    n_local = lax.axis_size("local")
    n_dev = n_node * n_local
    rows = expert_inputs.shape[1]
    cap = rows // n_dev
    tokens, width = output_grad.shape
    ff = w_in.shape[2]
    ids = expert_ids.reshape(1, tokens)
    place = slots.reshape(1, tokens)
    gate = gate_prob.reshape(1, tokens)
    anywhere = pl.BlockSpec(memory_space=pl.ANY)
    vmem = pl.BlockSpec(memory_space=pltpu.VMEM)
    part = n_dev // 2
    dma = pltpu.SemaphoreType.DMA
    back, hid_t, pg, x_t, routed = pl.pallas_call(
        functools.partial(exchange_kernel, n_node, n_local, cap),
        out_shape=[
            jax.ShapeDtypeStruct((n_dev, MSG, LANES), BF16),
            jax.ShapeDtypeStruct((ff, rows), BF16),
            jax.ShapeDtypeStruct((rows, ff), BF16),
            jax.ShapeDtypeStruct((width, rows), BF16),
            jax.ShapeDtypeStruct((rows, width), BF16),
        ],
        in_specs=[vmem] * 3 + [anywhere] * 4,
        out_specs=[anywhere] * 5,
        scratch_shapes=[
            pltpu.VMEM((tokens, width), BF16),
            pltpu.VMEM((rows, width), BF16),
            pltpu.VMEM((width, ff), BF16),
            pltpu.VMEM((ff, width), BF16),
            pltpu.VMEM((rows, width), BF16),
            pltpu.VMEM((width, rows), BF16),
            pltpu.VMEM((rows, ff), BF16),
            pltpu.VMEM((ff, rows), BF16),
            pltpu.VMEM((rows, ff), F32),
            pltpu.VMEM((rows, ff), BF16),
            pltpu.VMEM((rows, width), BF16),
            pltpu.VMEM((n_dev * MSG, LANES), F32),
            pltpu.VMEM((n_dev, MSG, LANES), BF16),
            pltpu.VMEM((2, part, MSG, LANES), BF16),
            pltpu.VMEM((2, part, MSG, LANES), BF16),
            dma((4,)),
            dma((4,)),
            dma,
            dma,
            dma((2,)),
            dma,
            dma,
        ],
        compiler_params=pltpu.CompilerParams(
            collective_id=0, has_side_effects=True, vmem_limit_bytes=VMEM_LIMIT
        ),
        name="exchange",
    )(ids, place, gate, output_grad, expert_inputs[0], w_in[0], w_out[0])

    tile = 512
    whole = lambda *shape: pl.BlockSpec(shape, lambda k: (0,) * len(shape))
    token_grad, gate_grad, in_grad, out_grad = pl.pallas_call(
        functools.partial(weights_kernel, cap),
        grid=(ff // tile,),
        out_shape=[
            jax.ShapeDtypeStruct((tokens, width), BF16),
            jax.ShapeDtypeStruct((1, tokens), F32),
            jax.ShapeDtypeStruct((width, ff), BF16),
            jax.ShapeDtypeStruct((ff, width), BF16),
        ],
        in_specs=[
            whole(1, tokens),
            whole(1, tokens),
            whole(1, tokens),
            whole(n_dev, MSG, LANES),
            pl.BlockSpec((tile, rows), lambda k: (k, 0)),
            pl.BlockSpec((rows, tile), lambda k: (0, k)),
            whole(width, rows),
            whole(rows, width),
        ],
        out_specs=[
            whole(tokens, width),
            whole(1, tokens),
            pl.BlockSpec((width, tile), lambda k: (0, k)),
            pl.BlockSpec((tile, width), lambda k: (k, 0)),
        ],
        scratch_shapes=[pltpu.VMEM((n_dev * MSG, LANES), F32), pltpu.VMEM((rows, width), BF16)],
        compiler_params=pltpu.CompilerParams(vmem_limit_bytes=VMEM_LIMIT),
        name="weights",
    )(ids, place, gate, back, hid_t, pg, x_t, routed)
    return (token_grad, gate_grad.reshape(tokens), in_grad[None], out_grad[None])


def solution(mesh):
    placed = (
        P(("node", "local"), None),
        P(("node", "local")),
        P(("node", "local")),
        P(("node", "local")),
        P(("node", "local"), None, None),
        P(("node", "local"), None, None),
        P(("node", "local"), None, None),
    )
    return jax.shard_map(
        shards,
        mesh=mesh,
        in_specs=placed,
        out_specs=(
            P(("node", "local"), None),
            P(("node", "local")),
            P(("node", "local"), None, None),
            P(("node", "local"), None, None),
        ),
        check_vma=False,
    )
```

time: 119 us -> 64.9 us (0.55)
  the two profiles are of different devices: /device:TPU:1 before, /device:TPU:3 now
where the time goes in v1:
time: 64.9 us; the launch traced here: 64.6 us
  Pallas kernels  63.9 us (98%)
    pallas_call x1, Pallas kernels, shards(): pl.pallas_call(functools.partial(exchange_kernel, n_node, n_local, cap),...  48.8 us
    pallas_call x1, Pallas kernels, shards(): pl.pallas_call(functools.partial(weights_kernel, cap), grid=(ff // tile,)...  15.2 us

profile of v1, /device:TPU:3, one launch (start us, length us, event | category | flops | bytes accessed | tf_op | source)
XLA Modules:
  0.0 64.6 jit_solution(13831189268675121614)
XLA Ops:
  0.6 48.8 %exchange.1 = (bf16[128,32,128]{2,1,0:T(8,128)(2,1)}, bf16[3072,640]{1,0:T(8,128)(2,1)}, bf16[640,3072]{1,0:T(8,128)(2,1)}, bf16[768,640]{1,0:T(8,128)(2,1)}, bf16[640,768]{1,0:T(8,128)(2,1)}) custom-call(s32[1,512]{1,0:T(1,128)} %bitcast.12, s32[1,512]{1,0:T(1,128)} %bitcast.14, f32[1,512]{1,0:T(1,128)} %bitcast.16, bf16[512,768]{1,0:T(8,128)(2,1)} %og_hbm.1, ...), custom_call_target="tpu_custom_call" | custom-call | tf_op jit(solution)/shard_map/exchange/pallas_call | solution.py:256
  49.4 15.2 %weights.1 = (bf16[512,768]{1,0:T(8,128)(2,1)}, f32[1,512]{1,0:T(1,128)}, bf16[768,3072]{1,0:T(8,128)(2,1)}, bf16[3072,768]{1,0:T(8,128)(2,1)}) custom-call(s32[1,512]{1,0:T(1,128)} %bitcast.13, s32[1,512]{1,0:T(1,128)} %bitcast.15, f32[1,512]{1,0:T(1,128)} %bitcast.17, bf16[128,32,128]{2,1,0:T(8,128)(2,1)} %get-tuple-element.13.back, ...), custom_call_target="tpu_custom_call" | custom-call | tf_op jit(solution)/shard_map/weights/pallas_call | solution.py:299

commit v2 on v1

--- a/solution.py
+++ b/solution.py
@@ -15,7 +15,10 @@
 MSG = 32
 NT = (((1,), (1,)), ((), ()))
 TN = (((0,), (0,)), ((), ()))
-VMEM_LIMIT = 60 * 1024 * 1024
+VMEM_LIMIT = 44 * 1024 * 1024
+FWD_TILE = 512
+BWD_TILE = 512
+GRAD_TILE = 512
 
 
 def signal(sem, device):
@@ -24,9 +27,9 @@
 
 def exchange_kernel(
     n_node, n_local, cap, ids, slots, gate, og_hbm, x_hbm, win_hbm, wout_hbm,
-    back, hid_t_hbm, pg_hbm, x_t_hbm, routed_hbm,
+    back, in_grad, out_grad,
     og, x, win, wout, xp, x_t, hid, hid_t, slope, pg, routed, wide, msg, recv, ret,
-    in_sem, out_sem, own_sem, send_sem, recv_sem, back_send_sem, back_recv_sem,
+    in_sem, own_sem, send_sem, recv_sem, back_send_sem, back_recv_sem,
 ):
     node, local = lax.axis_index("node"), lax.axis_index("local")
     n_dev = n_node * n_local
@@ -104,7 +107,8 @@
         xp[step * half : (step + 1) * half, :] = ordered
 
     loads[2].wait()
-    tile = 256
+    tile = FWD_TILE
+    wide_tile = GRAD_TILE
 
     def forward(k, carry):
         cols = pl.ds(pl.multiple_of(k * tile, tile), tile)
@@ -119,16 +123,9 @@
 
     lax.fori_loop(0, ff // tile, forward, 0)
     x_t[...] = xp[...].T
-    stores = [
-        pltpu.make_async_copy(src, dst, out_sem.at[k])
-        for k, (src, dst) in enumerate(
-            ((hid_t, hid_t_hbm), (x_t, x_t_hbm), (pg, pg_hbm), (routed, routed_hbm))
-        )
-    ]
-    stores[0].start()
-    stores[1].start()
     own.wait()
     loads[3].wait()
+    tile = BWD_TILE
 
     own_back = pltpu.make_async_copy(ret.at[0, place], back.at[me], own_sem)
     for step in range(2):
@@ -188,54 +185,67 @@
 
         lax.fori_loop(1 - step, part, reply, 0)
 
-    stores[2].start()
-    stores[3].start()
+    def out_tile(k, carry):
+        part_rows = pl.ds(pl.multiple_of(k * wide_tile, wide_tile), wide_tile)
+        out_grad[part_rows, :] = jnp.dot(
+            hid_t[part_rows, :], routed[...], preferred_element_type=F32
+        ).astype(BF16)
+        return carry
+
+    def in_tile(k, carry):
+        cols = pl.ds(pl.multiple_of(k * wide_tile, wide_tile), wide_tile)
+        in_grad[:, cols] = jnp.dot(x_t[...], pg[:, cols], preferred_element_type=F32).astype(BF16)
+        return carry
+
+    lax.fori_loop(0, ff // wide_tile, out_tile, 0)
+    lax.fori_loop(0, ff // wide_tile, in_tile, 0)
     sent = msg.at[pl.ds(0, n_dev - 1)]
     pltpu.make_async_copy(sent, sent, send_sem).wait()
     pltpu.make_async_copy(sent, sent, back_send_sem).wait()
     came = back.at[pl.ds(0, n_dev - 1)]
     own_back.wait()
-    for store in stores:
-        store.wait()
     pltpu.make_async_copy(came, came, back_recv_sem).wait()
 
 
-def weights_kernel(
-    cap, ids, slots, gate, back, hid_t, pg, x_t, routed, token_grad, gate_grad, in_grad, out_grad, wide, rows_back
+def combine_kernel(
+    cap, ids, slots, gate, back, in_vmem, out_vmem, token_grad, gate_grad, in_grad, out_grad, wide, rows_back, sem
 ):
-    out_grad[...] = jnp.dot(hid_t[...], routed[...], preferred_element_type=F32).astype(BF16)
-    in_grad[...] = jnp.dot(x_t[...], pg[...], preferred_element_type=F32).astype(BF16)
-
-    @pl.when(pl.program_id(0) == 0)
-    def _():
-        n_dev = back.shape[0]
-        tokens, width = token_grad.shape
-        blocks = width // LANES
-        wide[...] = back[...].astype(F32).reshape(n_dev * MSG, LANES)
-        for c in range(cap):
-            for b in range(blocks):
-                rows_back[c * n_dev : (c + 1) * n_dev, b * LANES : (b + 1) * LANES] = wide[
-                    pl.ds(c * blocks + b, n_dev, stride=MSG), :
-                ].astype(BF16)
-        high = wide[pl.ds(cap * blocks, n_dev, stride=MSG), :].astype(BF16)
-        low = wide[pl.ds(cap * blocks + 1, n_dev, stride=MSG), :].astype(BF16)
-        target = jnp.where(slots[...] >= 0, slots[...] * n_dev + ids[...], -1)
-        column = jnp.broadcast_to(target.astype(F32), (LANES, tokens)).T
-        lane = lax.broadcasted_iota(jnp.int32, (tokens, LANES), 1).astype(F32)
-        hits = [
-            jnp.where(column == lane + (k * LANES), 1.0, 0.0).astype(BF16)
-            for k in range(cap * n_dev // LANES)
-        ]
-        token_grad[...] = jnp.dot(
-            jnp.concatenate(hits, axis=1), rows_back[...], preferred_element_type=F32
-        ).astype(BF16)
-        expert = lax.broadcasted_iota(jnp.int32, (n_dev, tokens), 0) == ids[...]
-        expert = expert.astype(BF16)
-        products = lax.dot_general(high, expert, TN, preferred_element_type=F32)
-        products += lax.dot_general(low, expert, TN, preferred_element_type=F32)
-        chosen = lax.broadcasted_iota(jnp.int32, (LANES, tokens), 0) == slots[...]
-        picked = jnp.sum(jnp.where(chosen, products, 0.0)[0:8], axis=0, keepdims=True)
-        gate_grad[...] = picked / gate[...]
+    copies = [
+        pltpu.make_async_copy(in_vmem, in_grad, sem.at[0]),
+        pltpu.make_async_copy(out_vmem, out_grad, sem.at[1]),
+    ]
+    for copy in copies:
+        copy.start()
+    n_dev = back.shape[0]
+    tokens, width = token_grad.shape
+    blocks = width // LANES
+    wide[...] = back[...].astype(F32).reshape(n_dev * MSG, LANES)
+    for c in range(cap):
+        for b in range(blocks):
+            rows_back[c * n_dev : (c + 1) * n_dev, b * LANES : (b + 1) * LANES] = wide[
+                pl.ds(c * blocks + b, n_dev, stride=MSG), :
+            ].astype(BF16)
+    high = wide[pl.ds(cap * blocks, n_dev, stride=MSG), :].astype(BF16)
+    low = wide[pl.ds(cap * blocks + 1, n_dev, stride=MSG), :].astype(BF16)
+    target = jnp.where(slots[...] >= 0, slots[...] * n_dev + ids[...], -1)
+    column = jnp.broadcast_to(target.astype(F32), (LANES, tokens)).T
+    lane = lax.broadcasted_iota(jnp.int32, (tokens, LANES), 1).astype(F32)
+    hits = [
+        jnp.where(column == lane + (k * LANES), 1.0, 0.0).astype(BF16)
+        for k in range(cap * n_dev // LANES)
+    ]
+    token_grad[...] = jnp.dot(
+        jnp.concatenate(hits, axis=1), rows_back[...], preferred_element_type=F32
+    ).astype(BF16)
+    expert = lax.broadcasted_iota(jnp.int32, (n_dev, tokens), 0) == ids[...]
+    expert = expert.astype(BF16)
+    products = lax.dot_general(high, expert, TN, preferred_element_type=F32)
+    products += lax.dot_general(low, expert, TN, preferred_element_type=F32)
+    chosen = lax.broadcasted_iota(jnp.int32, (LANES, tokens), 0) == slots[...]
+    picked = jnp.sum(jnp.where(chosen, products, 0.0)[0:8], axis=0, keepdims=True)
+    gate_grad[...] = picked / gate[...]
+    for copy in copies:
+        copy.wait()
 
 
 def shards(output_grad, gate_prob, expert_ids, slots, expert_inputs, w_in, w_out):
@@ -253,17 +263,15 @@
     vmem = pl.BlockSpec(memory_space=pltpu.VMEM)
     part = n_dev // 2
     dma = pltpu.SemaphoreType.DMA
-    back, hid_t, pg, x_t, routed = pl.pallas_call(
+    back, in_vmem, out_vmem = pl.pallas_call(
         functools.partial(exchange_kernel, n_node, n_local, cap),
         out_shape=[
-            jax.ShapeDtypeStruct((n_dev, MSG, LANES), BF16),
-            jax.ShapeDtypeStruct((ff, rows), BF16),
-            jax.ShapeDtypeStruct((rows, ff), BF16),
-            jax.ShapeDtypeStruct((width, rows), BF16),
-            jax.ShapeDtypeStruct((rows, width), BF16),
+            pltpu.VMEM((n_dev, MSG, LANES), BF16),
+            pltpu.VMEM((width, ff), BF16),
+            pltpu.VMEM((ff, width), BF16),
         ],
         in_specs=[vmem] * 3 + [anywhere] * 4,
-        out_specs=[anywhere] * 5,
+        out_specs=[vmem] * 3,
         scratch_shapes=[
             pltpu.VMEM((tokens, width), BF16),
             pltpu.VMEM((rows, width), BF16),
@@ -281,7 +289,6 @@
             pltpu.VMEM((2, part, MSG, LANES), BF16),
             pltpu.VMEM((2, part, MSG, LANES), BF16),
             dma((4,)),
-            dma((4,)),
             dma,
             dma,
             dma((2,)),
@@ -294,37 +301,24 @@
         name="exchange",
     )(ids, place, gate, output_grad, expert_inputs[0], w_in[0], w_out[0])
 
-    tile = 512
-    whole = lambda *shape: pl.BlockSpec(shape, lambda k: (0,) * len(shape))
     token_grad, gate_grad, in_grad, out_grad = pl.pallas_call(
-        functools.partial(weights_kernel, cap),
-        grid=(ff // tile,),
+        functools.partial(combine_kernel, cap),
         out_shape=[
             jax.ShapeDtypeStruct((tokens, width), BF16),
             jax.ShapeDtypeStruct((1, tokens), F32),
             jax.ShapeDtypeStruct((width, ff), BF16),
             jax.ShapeDtypeStruct((ff, width), BF16),
         ],
-        in_specs=[
-            whole(1, tokens),
-            whole(1, tokens),
-            whole(1, tokens),
-            whole(n_dev, MSG, LANES),
-            pl.BlockSpec((tile, rows), lambda k: (k, 0)),
-            pl.BlockSpec((rows, tile), lambda k: (0, k)),
-            whole(width, rows),
-            whole(rows, width),
+        in_specs=[vmem] * 6,
+        out_specs=[vmem, vmem, anywhere, anywhere],
+        scratch_shapes=[
+            pltpu.VMEM((n_dev * MSG, LANES), F32),
+            pltpu.VMEM((rows, width), BF16),
+            dma((2,)),
         ],
-        out_specs=[
-            whole(tokens, width),
-            whole(1, tokens),
-            pl.BlockSpec((width, tile), lambda k: (0, k)),
-            pl.BlockSpec((tile, width), lambda k: (k, 0)),
-        ],
-        scratch_shapes=[pltpu.VMEM((n_dev * MSG, LANES), F32), pltpu.VMEM((rows, width), BF16)],
-        compiler_params=pltpu.CompilerParams(vmem_limit_bytes=VMEM_LIMIT),
-        name="weights",
-    )(ids, place, gate, back, hid_t, pg, x_t, routed)
+        compiler_params=pltpu.CompilerParams(vmem_limit_bytes=16 * 1024 * 1024),
+        name="combine",
+    )(ids, place, gate, back, in_vmem, out_vmem)
     return (token_grad, gate_grad.reshape(tokens), in_grad[None], out_grad[None])
 
 

time: 64.9 us -> 52.4 us (0.81)
  the two profiles are of different devices: /device:TPU:3 before, /device:TPU:1 now
where the time goes in v2:
time: 52.4 us; the launch traced here: 51.4 us
  Pallas kernels  50.7 us (97%)
  between operations  0.69 us (1%)
    pallas_call x1, Pallas kernels, shards(): pl.pallas_call(functools.partial(exchange_kernel, n_node, n_local, cap),...  45.5 us
    pallas_call x1, Pallas kernels, shards(): pl.pallas_call(functools.partial(combine_kernel, cap), out_shape=[jax.Sha...  5.17 us

profile of v2, /device:TPU:1, one launch (start us, length us, event | category | flops | bytes accessed | tf_op | source)
XLA Modules:
  0.0 51.4 jit_solution(13286762000288447295)
XLA Ops:
  0.6 0.0 copy-start
  0.6 0.0 copy-start.1
  0.7 0.0 copy-start.2
  0.7 45.5 %exchange.1 = (bf16[128,32,128]{2,1,0:T(8,128)(2,1)S(1)}, bf16[768,3072]{1,0:T(8,128)(2,1)S(1)}, bf16[3072,768]{1,0:T(8,128)(2,1)S(1)}) custom-call(s32[1,512]{1,0:T(1,128)} %bitcast.9, s32[1,512]{1,0:T(1,128)} %bitcast.11, f32[1,512]{1,0:T(1,128)} %bitcast.13, bf16[512,768]{1,0:T(8,128)(2,1)} %og_hbm.1, bf16[640,768]{1,0:T(8,128)(2,1)} %bitcast.17, ...), custom_call_target="tpu_custom_call" | custom-call | tf_op jit(solution)/shard_map/exchange/pallas_call | solution.py:266
  46.2 0.0 copy-done
  46.2 0.0 copy-done.1
  46.2 0.0 copy-done.2
  46.2 5.2 %combine.1 = (bf16[512,768]{1,0:T(8,128)(2,1)}, f32[1,512]{1,0:T(1,128)}, bf16[768,3072]{1,0:T(8,128)(2,1)}, bf16[3072,768]{1,0:T(8,128)(2,1)}) custom-call(s32[1,512]{1,0:T(1,128)S(1)} %bitcast.10, s32[1,512]{1,0:T(1,128)S(1)} %bitcast.12, f32[1,512]{1,0:T(1,128)S(1)} %bitcast.14, bf16[128,32,128]{2,1,0:T(8,128)(2,1)S(1)} %get-tuple-element.11.back, ...), custom_call_target="tpu_custom_call" | custom-call | tf_op jit(solution)/shard_map/combine/pallas_call | solution.py:304
Async XLA Ops:
  0.6 45.6 %copy-start = (s32[512]{0:T(512)S(1)}, s32[512]{0:T(512)}, u32[]{:S(2)}) copy-start(s32[512]{0:T(512)} %param.9) | copy-start | bytes 6148
  0.6 45.6 %copy-start.1 = (s32[512]{0:T(512)S(1)}, s32[512]{0:T(512)}, u32[]{:S(2)}) copy-start(s32[512]{0:T(512)} %param.10) | copy-start | bytes 6148
  0.7 45.6 %copy-start.2 = (f32[512]{0:T(512)S(1)}, f32[512]{0:T(512)}, u32[]{:S(2)}) copy-start(f32[512]{0:T(512)} %param.8) | copy-start | bytes 6148

commit v3 on v2

--- a/solution.py
+++ b/solution.py
@@ -16,9 +16,9 @@
 NT = (((1,), (1,)), ((), ()))
 TN = (((0,), (0,)), ((), ()))
 VMEM_LIMIT = 44 * 1024 * 1024
-FWD_TILE = 512
-BWD_TILE = 512
-GRAD_TILE = 512
+FWD_TILE = 1536
+BWD_TILE = 3072
+GRAD_TILE = 3072
 
 
 def signal(sem, device):
@@ -28,7 +28,7 @@
 def exchange_kernel(
     n_node, n_local, cap, ids, slots, gate, og_hbm, x_hbm, win_hbm, wout_hbm,
     back, in_grad, out_grad,
-    og, x, win, wout, xp, x_t, hid, hid_t, slope, pg, routed, wide, msg, recv, ret,
+    og, x, win, wout, xp, x_t, hid, slope, pg, routed, wide, msg, recv, ret,
     in_sem, own_sem, send_sem, recv_sem, back_send_sem, back_recv_sem,
 ):
     node, local = lax.axis_index("node"), lax.axis_index("local")
@@ -57,7 +57,8 @@
             signal(barrier, ((node + k) % n_node, j))
         return carry
 
-    lax.fori_loop(1, n_node, greet, 0)
+    for k in range(1, n_node):
+        greet(k, 0)
     for j in range(1, n_local):
         signal(barrier, (node, (local + j) % n_local))
 
@@ -81,21 +82,19 @@
 
     own = pltpu.make_async_copy(msg.at[me], recv.at[0, place], own_sem)
     own.start()
-    for step in range(2):
-
-        def send(k, carry, step=step):
-            to_node, to_local, there = peer(step, k)
-            pltpu.make_async_remote_copy(
-                src_ref=msg.at[to_node * n_local + to_local],
-                dst_ref=recv.at[step, place],
-                send_sem=send_sem,
-                recv_sem=recv_sem.at[step],
-                device_id=(to_node, to_local),
-                device_id_type=MESH,
-            ).start()
-            return carry
-
-        lax.fori_loop(1 - step, part, send, 0)
+    def send(step, k):
+        to_node, to_local, there = peer(step, k)
+        pltpu.make_async_remote_copy(
+            src_ref=msg.at[to_node * n_local + to_local],
+            dst_ref=recv.at[step, place],
+            send_sem=send_sem,
+            recv_sem=recv_sem.at[step],
+            device_id=(to_node, to_local),
+            device_id_type=MESH,
+        ).start()
+
+    for k in range(1, part):
+        send(0, k)
 
     loads[1].wait()
     for step in range(2):
@@ -111,18 +110,20 @@
     wide_tile = GRAD_TILE
 
     def forward(k, carry):
-        cols = pl.ds(pl.multiple_of(k * tile, tile), tile)
+        cols = pl.ds(k * tile if isinstance(k, int) else pl.multiple_of(k * tile, tile), tile)
         pre = jnp.dot(xp[...], win[:, cols], preferred_element_type=F32)
         cdf = 0.5 * (1.0 + lax.erf(pre * (1.0 / math.sqrt(2.0))))
         dens = jnp.exp(-0.5 * pre * pre) * (1.0 / math.sqrt(2.0 * math.pi))
         hidden = (pre * cdf).astype(BF16)
         hid[:, cols] = hidden
-        hid_t[cols, :] = hidden.T
         slope[:, cols] = cdf + pre * dens
         return carry
 
-    lax.fori_loop(0, ff // tile, forward, 0)
-    x_t[...] = xp[...].T
+    n_tiles = ff // tile
+    for t in range(n_tiles):
+        forward(t, 0)
+    for k in range(part):
+        send(1, k)
     own.wait()
     loads[3].wait()
     tile = BWD_TILE
@@ -141,7 +142,7 @@
                 )
 
         def backward(k, total, mine=mine):
-            cols = pl.ds(pl.multiple_of(k * tile, tile), tile)
+            cols = pl.ds(k * tile if isinstance(k, int) else pl.multiple_of(k * tile, tile), tile)
             up = lax.dot_general(routed[mine, :], wout[cols, :], NT, preferred_element_type=F32)
             pg[mine, cols] = (up * slope[mine, cols]).astype(BF16)
             both = up * hid[mine, cols].astype(F32)
@@ -183,14 +184,17 @@
             ).start()
             return carry
 
-        lax.fori_loop(1 - step, part, reply, 0)
+        for k in range(1 - step, part):
+            reply(k, 0)
 
     def out_tile(k, carry):
         part_rows = pl.ds(pl.multiple_of(k * wide_tile, wide_tile), wide_tile)
-        out_grad[part_rows, :] = jnp.dot(
-            hid_t[part_rows, :], routed[...], preferred_element_type=F32
+        out_grad[part_rows, :] = lax.dot_general(
+            hid[:, part_rows], routed[...], TN, preferred_element_type=F32
         ).astype(BF16)
         return carry
+
+    x_t[...] = xp[...].T
 
     def in_tile(k, carry):
         cols = pl.ds(pl.multiple_of(k * wide_tile, wide_tile), wide_tile)
@@ -280,7 +284,6 @@
             pltpu.VMEM((rows, width), BF16),
             pltpu.VMEM((width, rows), BF16),
             pltpu.VMEM((rows, ff), BF16),
-            pltpu.VMEM((ff, rows), BF16),
             pltpu.VMEM((rows, ff), F32),
             pltpu.VMEM((rows, ff), BF16),
             pltpu.VMEM((rows, width), BF16),

time: 52.4 us -> 46.9 us (0.90); the launches traced: 51.4 us -> 46.8 us
  Pallas kernels: 50.7 us -> 45.9 us
    pallas_call x1, Pallas kernels: 45.5 us -> 40.7 us  [shards(): pl.pallas_call(functools.partial(exchange_kernel, n_node, n_local, cap),...]
where the time goes in v3:
time: 46.9 us; the launch traced here: 46.8 us
  Pallas kernels  45.9 us (98%)
  between operations  0.87 us (2%)
    pallas_call x1, Pallas kernels, shards(): pl.pallas_call(functools.partial(exchange_kernel, n_node, n_local, cap),...  40.7 us
    pallas_call x1, Pallas kernels, shards(): pl.pallas_call(functools.partial(combine_kernel, cap), out_shape=[jax.Sha...  5.17 us

profile of v3, /device:TPU:1, one launch (start us, length us, event | category | flops | bytes accessed | tf_op | source)
XLA Modules:
  0.0 46.8 jit_solution(7297347099225309687)
XLA Ops:
  0.6 0.0 copy-start
  0.6 0.0 copy-start.1
  0.7 0.0 copy-start.2
  0.7 40.7 %exchange.1 = (bf16[128,32,128]{2,1,0:T(8,128)(2,1)S(1)}, bf16[768,3072]{1,0:T(8,128)(2,1)S(1)}, bf16[3072,768]{1,0:T(8,128)(2,1)S(1)}) custom-call(s32[1,512]{1,0:T(1,128)} %bitcast.9, s32[1,512]{1,0:T(1,128)} %bitcast.11, f32[1,512]{1,0:T(1,128)} %bitcast.13, bf16[512,768]{1,0:T(8,128)(2,1)} %og_hbm.1, bf16[640,768]{1,0:T(8,128)(2,1)} %bitcast.17, ...), custom_call_target="tpu_custom_call" | custom-call | tf_op jit(solution)/shard_map/exchange/pallas_call | solution.py:270
  41.4 0.0 copy-done
  41.4 0.0 copy-done.1
  41.4 0.0 copy-done.2
  41.4 5.2 %combine.1 = (bf16[512,768]{1,0:T(8,128)(2,1)}, f32[1,512]{1,0:T(1,128)}, bf16[768,3072]{1,0:T(8,128)(2,1)}, bf16[3072,768]{1,0:T(8,128)(2,1)}) custom-call(s32[1,512]{1,0:T(1,128)S(1)} %bitcast.10, s32[1,512]{1,0:T(1,128)S(1)} %bitcast.12, f32[1,512]{1,0:T(1,128)S(1)} %bitcast.14, bf16[128,32,128]{2,1,0:T(8,128)(2,1)S(1)} %get-tuple-element.11.back, ...), custom_call_target="tpu_custom_call" | custom-call | tf_op jit(solution)/shard_map/combine/pallas_call | solution.py:307
Async XLA Ops:
  0.6 40.8 %copy-start = (s32[512]{0:T(512)S(1)}, s32[512]{0:T(512)}, u32[]{:S(2)}) copy-start(s32[512]{0:T(512)} %param.9) | copy-start | bytes 6148
  0.6 40.8 %copy-start.1 = (s32[512]{0:T(512)S(1)}, s32[512]{0:T(512)}, u32[]{:S(2)}) copy-start(s32[512]{0:T(512)} %param.10) | copy-start | bytes 6148
  0.7 40.8 %copy-start.2 = (f32[512]{0:T(512)S(1)}, f32[512]{0:T(512)}, u32[]{:S(2)}) copy-start(f32[512]{0:T(512)} %param.8) | copy-start | bytes 6148

commit v4 on v3

--- a/solution.py
+++ b/solution.py
@@ -26,9 +26,9 @@
 
 
 def exchange_kernel(
-    n_node, n_local, cap, ids, slots, gate, og_hbm, x_hbm, win_hbm, wout_hbm,
+    n_node, n_local, cap, ids_hbm, slots_hbm, gate_hbm, og_hbm, x_hbm, win_hbm, wout_hbm,
     back, in_grad, out_grad,
-    og, x, win, wout, xp, x_t, hid, slope, pg, routed, wide, msg, recv, ret,
+    ids, slots, gate, og, x, win, wout, xp, x_t, hid, slope, pg, routed, wide, msg, recv, ret,
     in_sem, own_sem, send_sem, recv_sem, back_send_sem, back_recv_sem,
 ):
     node, local = lax.axis_index("node"), lax.axis_index("local")
@@ -45,9 +45,20 @@
 
     loads = [
         pltpu.make_async_copy(src, dst, in_sem.at[k])
-        for k, (src, dst) in enumerate(((og_hbm, og), (x_hbm, x), (win_hbm, win), (wout_hbm, wout)))
+        for k, (src, dst) in enumerate(
+            (
+                (og_hbm, og),
+                (x_hbm, x),
+                (win_hbm, win),
+                (wout_hbm, wout),
+                (ids_hbm, ids),
+                (slots_hbm, slots),
+                (gate_hbm, gate),
+            )
+        )
     ]
-    for load in loads:
+    early = (loads[4], loads[5], loads[6], loads[0])
+    for load in early:
         load.start()
 
     barrier = pltpu.get_barrier_semaphore()
@@ -62,7 +73,10 @@
     for j in range(1, n_local):
         signal(barrier, (node, (local + j) % n_local))
 
-    loads[0].wait()
+    for load in early:
+        load.wait()
+    for load in loads[1:4]:
+        load.start()
     target = jnp.where(slots[...] >= 0, slots[...] * n_dev + ids[...], -1)
     tokens = target.shape[1]
     for c in range(cap):
@@ -212,7 +226,7 @@
 
 
 def combine_kernel(
-    cap, ids, slots, gate, back, in_vmem, out_vmem, token_grad, gate_grad, in_grad, out_grad, wide, rows_back, sem
+    cap, ids, slots, gate, back, in_vmem, out_vmem, token_hbm, gate_grad, in_grad, out_grad, wide, rows_back, token_grad, sem
 ):
     copies = [
         pltpu.make_async_copy(in_vmem, in_grad, sem.at[0]),
@@ -241,6 +255,8 @@
     token_grad[...] = jnp.dot(
         jnp.concatenate(hits, axis=1), rows_back[...], preferred_element_type=F32
     ).astype(BF16)
+    copies.append(pltpu.make_async_copy(token_grad, token_hbm, sem.at[2]))
+    copies[2].start()
     expert = lax.broadcasted_iota(jnp.int32, (n_dev, tokens), 0) == ids[...]
     expert = expert.astype(BF16)
     products = lax.dot_general(high, expert, TN, preferred_element_type=F32)
@@ -274,9 +290,12 @@
             pltpu.VMEM((width, ff), BF16),
             pltpu.VMEM((ff, width), BF16),
         ],
-        in_specs=[vmem] * 3 + [anywhere] * 4,
+        in_specs=[anywhere] * 7,
         out_specs=[vmem] * 3,
         scratch_shapes=[
+            pltpu.VMEM((1, tokens), jnp.int32),
+            pltpu.VMEM((1, tokens), jnp.int32),
+            pltpu.VMEM((1, tokens), F32),
             pltpu.VMEM((tokens, width), BF16),
             pltpu.VMEM((rows, width), BF16),
             pltpu.VMEM((width, ff), BF16),
@@ -291,7 +310,7 @@
             pltpu.VMEM((n_dev, MSG, LANES), BF16),
             pltpu.VMEM((2, part, MSG, LANES), BF16),
             pltpu.VMEM((2, part, MSG, LANES), BF16),
-            dma((4,)),
+            dma((7,)),
             dma,
             dma,
             dma((2,)),
@@ -313,11 +332,12 @@
             jax.ShapeDtypeStruct((ff, width), BF16),
         ],
         in_specs=[vmem] * 6,
-        out_specs=[vmem, vmem, anywhere, anywhere],
+        out_specs=[anywhere, vmem, anywhere, anywhere],
         scratch_shapes=[
             pltpu.VMEM((n_dev * MSG, LANES), F32),
             pltpu.VMEM((rows, width), BF16),
-            dma((2,)),
+            pltpu.VMEM((tokens, width), BF16),
+            dma((3,)),
         ],
         compiler_params=pltpu.CompilerParams(vmem_limit_bytes=16 * 1024 * 1024),
         name="combine",

time: 46.9 us -> 46.1 us (0.983)
  Pallas kernels: 45.9 us -> 45.1 us
    pallas_call x1, Pallas kernels: 40.7 us -> 40.1 us  [shards(): pl.pallas_call(functools.partial(exchange_kernel, n_node, n_local, cap),...]
where the time goes in v4:
time: 46.1 us; the launch traced here: 46 us
  Pallas kernels  45.1 us (98%)
  between operations  0.87 us (2%)
    pallas_call x1, Pallas kernels, shards(): pl.pallas_call(functools.partial(exchange_kernel, n_node, n_local, cap),...  40.1 us
    pallas_call x1, Pallas kernels, shards(): pl.pallas_call(functools.partial(combine_kernel, cap), out_shape=[jax.Sha...  4.99 us

profile of v4, /device:TPU:1, one launch (start us, length us, event | category | flops | bytes accessed | tf_op | source)
XLA Modules:
  0.0 46.0 jit_solution(11912517761924351342)
XLA Ops:
  0.6 0.0 copy-start
  0.6 0.0 copy-start.1
  0.7 0.0 copy-start.2
  0.7 40.1 %exchange.1 = (bf16[128,32,128]{2,1,0:T(8,128)(2,1)S(1)}, bf16[768,3072]{1,0:T(8,128)(2,1)S(1)}, bf16[3072,768]{1,0:T(8,128)(2,1)S(1)}) custom-call(s32[1,512]{1,0:T(1,128)} %bitcast.9, s32[1,512]{1,0:T(1,128)} %bitcast.11, f32[1,512]{1,0:T(1,128)} %bitcast.13, bf16[512,768]{1,0:T(8,128)(2,1)} %og_hbm.1, bf16[640,768]{1,0:T(8,128)(2,1)} %bitcast.17, ...), custom_call_target="tpu_custom_call" | custom-call | tf_op jit(solution)/shard_map/exchange/pallas_call | solution.py:286
  40.8 0.0 copy-done
  40.8 0.0 copy-done.1
  40.8 0.0 copy-done.2
  40.8 5.0 %combine.1 = (bf16[512,768]{1,0:T(8,128)(2,1)}, f32[1,512]{1,0:T(1,128)}, bf16[768,3072]{1,0:T(8,128)(2,1)}, bf16[3072,768]{1,0:T(8,128)(2,1)}) custom-call(s32[1,512]{1,0:T(1,128)S(1)} %bitcast.10, s32[1,512]{1,0:T(1,128)S(1)} %bitcast.12, f32[1,512]{1,0:T(1,128)S(1)} %bitcast.14, bf16[128,32,128]{2,1,0:T(8,128)(2,1)S(1)} %get-tuple-element.11.back, ...), custom_call_target="tpu_custom_call" | custom-call | tf_op jit(solution)/shard_map/combine/pallas_call | solution.py:326
Async XLA Ops:
  0.6 40.2 %copy-start = (s32[512]{0:T(512)S(1)}, s32[512]{0:T(512)}, u32[]{:S(2)}) copy-start(s32[512]{0:T(512)} %param.9) | copy-start | bytes 6148
  0.6 40.2 %copy-start.1 = (s32[512]{0:T(512)S(1)}, s32[512]{0:T(512)}, u32[]{:S(2)}) copy-start(s32[512]{0:T(512)} %param.10) | copy-start | bytes 6148
  0.7 40.2 %copy-start.2 = (f32[512]{0:T(512)S(1)}, f32[512]{0:T(512)}, u32[]{:S(2)}) copy-start(f32[512]{0:T(512)} %param.8) | copy-start | bytes 6148

commit v5 on v4

--- a/solution.py
+++ b/solution.py
@@ -226,7 +226,7 @@
 
 
 def combine_kernel(
-    cap, ids, slots, gate, back, in_vmem, out_vmem, token_hbm, gate_grad, in_grad, out_grad, wide, rows_back, token_grad, sem
+    cap, ids, slots, gate, back, in_vmem, out_vmem, token_hbm, gate_hbm, in_grad, out_grad, wide, rows_back, token_grad, gate_grad, sem
 ):
     copies = [
         pltpu.make_async_copy(in_vmem, in_grad, sem.at[0]),
@@ -264,6 +264,8 @@
     chosen = lax.broadcasted_iota(jnp.int32, (LANES, tokens), 0) == slots[...]
     picked = jnp.sum(jnp.where(chosen, products, 0.0)[0:8], axis=0, keepdims=True)
     gate_grad[...] = picked / gate[...]
+    copies.append(pltpu.make_async_copy(gate_grad, gate_hbm, sem.at[3]))
+    copies[3].start()
     for copy in copies:
         copy.wait()
 
@@ -332,12 +334,13 @@
             jax.ShapeDtypeStruct((ff, width), BF16),
         ],
         in_specs=[vmem] * 6,
-        out_specs=[anywhere, vmem, anywhere, anywhere],
+        out_specs=[anywhere] * 4,
         scratch_shapes=[
             pltpu.VMEM((n_dev * MSG, LANES), F32),
             pltpu.VMEM((rows, width), BF16),
             pltpu.VMEM((tokens, width), BF16),
-            dma((3,)),
+            pltpu.VMEM((1, tokens), F32),
+            dma((4,)),
         ],
         compiler_params=pltpu.CompilerParams(vmem_limit_bytes=16 * 1024 * 1024),
         name="combine",

time: 46.1 us -> 45 us (0.976)
  Pallas kernels: 45.1 us -> 44 us
    pallas_call x1, Pallas kernels: 4.99 us -> 3.89 us  [shards(): pl.pallas_call(functools.partial(combine_kernel, cap), out_shape=[jax.Sha...]
where the time goes in v5:
time: 45 us; the launch traced here: 44.9 us
  Pallas kernels  44 us (98%)
  between operations  0.87 us (2%)
    pallas_call x1, Pallas kernels, shards(): pl.pallas_call(functools.partial(exchange_kernel, n_node, n_local, cap),...  40.1 us
    pallas_call x1, Pallas kernels, shards(): pl.pallas_call(functools.partial(combine_kernel, cap), out_shape=[jax.Sha...  3.89 us

profile of v5, /device:TPU:1, one launch (start us, length us, event | category | flops | bytes accessed | tf_op | source)
XLA Modules:
  0.0 44.9 jit_solution(14470267701713571198)
XLA Ops:
  0.6 0.0 copy-start
  0.6 0.0 copy-start.1
  0.7 0.0 copy-start.2
  0.7 40.1 %exchange.1 = (bf16[128,32,128]{2,1,0:T(8,128)(2,1)S(1)}, bf16[768,3072]{1,0:T(8,128)(2,1)S(1)}, bf16[3072,768]{1,0:T(8,128)(2,1)S(1)}) custom-call(s32[1,512]{1,0:T(1,128)} %bitcast.9, s32[1,512]{1,0:T(1,128)} %bitcast.11, f32[1,512]{1,0:T(1,128)} %bitcast.13, bf16[512,768]{1,0:T(8,128)(2,1)} %og_hbm.1, bf16[640,768]{1,0:T(8,128)(2,1)} %bitcast.17, ...), custom_call_target="tpu_custom_call" | custom-call | tf_op jit(solution)/shard_map/exchange/pallas_call | solution.py:288
  40.8 0.0 copy-done
  40.8 0.0 copy-done.1
  40.8 0.0 copy-done.2
  40.8 3.9 %combine.1 = (bf16[512,768]{1,0:T(8,128)(2,1)}, f32[1,512]{1,0:T(1,128)}, bf16[768,3072]{1,0:T(8,128)(2,1)}, bf16[3072,768]{1,0:T(8,128)(2,1)}) custom-call(s32[1,512]{1,0:T(1,128)S(1)} %bitcast.10, s32[1,512]{1,0:T(1,128)S(1)} %bitcast.12, f32[1,512]{1,0:T(1,128)S(1)} %bitcast.14, bf16[128,32,128]{2,1,0:T(8,128)(2,1)S(1)} %get-tuple-element.11.back, ...), custom_call_target="tpu_custom_call" | custom-call | tf_op jit(solution)/shard_map/combine/pallas_call | solution.py:328
Async XLA Ops:
  0.6 40.2 %copy-start = (s32[512]{0:T(512)S(1)}, s32[512]{0:T(512)}, u32[]{:S(2)}) copy-start(s32[512]{0:T(512)} %param.9) | copy-start | bytes 6148
  0.6 40.2 %copy-start.1 = (s32[512]{0:T(512)S(1)}, s32[512]{0:T(512)}, u32[]{:S(2)}) copy-start(s32[512]{0:T(512)} %param.10) | copy-start | bytes 6148
  0.7 40.2 %copy-start.2 = (f32[512]{0:T(512)S(1)}, f32[512]{0:T(512)}, u32[]{:S(2)}) copy-start(f32[512]{0:T(512)} %param.8) | copy-start | bytes 6148
